TPU v7x, 32 devices: a whole 2x2x4 slice. The times are simulated.
32 devices in a mesh: dp: 16 (over z, y, x), head: 2 (over core).
Axes of the slice: x: 2, y: 2, z: 4, core: 2. Of those that a mesh axis runs over, the one named last changes fastest.
Arguments:
- tokens: bfloat16 [16384, 768], P('dp'), may hold values from -6 to 6
- row_bucket: int32 [16], P('dp'), may hold values from 0 to 2, as said below
- row_lengths: int32 [16, 8], P('dp'), may hold values from 0 to 512, as said below
- teacher_query_weight: bfloat16 [768, 768], P(None, 'head'), may hold values from -0.21875 to 0.21875
- teacher_query_bias: float32 [768], P('head'), may hold values from -1.8 to 1.8
- teacher_key_weight: bfloat16 [768, 768], P(None, 'head'), may hold values from -0.21875 to 0.21875
- teacher_value_weight: bfloat16 [768, 768], P(None, 'head'), may hold values from -0.21875 to 0.21875
- teacher_value_bias: float32 [768], P('head'), may hold values from -1.8 to 1.8
- teacher_output_weight: bfloat16 [768, 768], P('head'), may hold values from -0.875 to 0.875
- teacher_output_bias: float32 [768], replicated, may hold values from -1.8 to 1.8
- teacher_first_gain: float32 [768], replicated, may hold values from 0.5 to 1.5
- teacher_first_shift: float32 [768], replicated, may hold values from -1.8 to 1.8
- teacher_hidden_weight: bfloat16 [768, 3072], P(None, 'head'), may hold values from -0.21875 to 0.21875
- teacher_hidden_bias: float32 [3072], P('head'), may hold values from -3 to 3
- teacher_return_weight: bfloat16 [3072, 768], P('head'), may hold values from -0.15625 to 0.15625
- teacher_return_bias: float32 [768], replicated, may hold values from -1.8 to 1.8
- teacher_second_gain: float32 [768], replicated, may hold values from 0.5 to 1.5
- teacher_second_shift: float32 [768], replicated, may hold values from -1.8 to 1.8
- student_query_weight: bfloat16 [768, 768], P(None, 'head'), may hold values from -0.21875 to 0.21875
- student_query_bias: float32 [768], P('head'), may hold values from -1.8 to 1.8
- student_key_weight: bfloat16 [768, 768], P(None, 'head'), may hold values from -0.21875 to 0.21875
- student_value_weight: bfloat16 [768, 768], P(None, 'head'), may hold values from -0.21875 to 0.21875
- student_value_bias: float32 [768], P('head'), may hold values from -1.8 to 1.8
- student_output_weight: bfloat16 [768, 768], P('head'), may hold values from -0.875 to 0.875
- student_output_bias: float32 [768], replicated, may hold values from -1.8 to 1.8
- student_first_gain: float32 [768], replicated, may hold values from 0.5 to 1.5
- student_first_shift: float32 [768], replicated, may hold values from -1.8 to 1.8
- student_hidden_weight: bfloat16 [768, 3072], P(None, 'head'), may hold values from -0.21875 to 0.21875
- student_hidden_bias: float32 [3072], P('head'), may hold values from -3 to 3
- student_return_weight: bfloat16 [3072, 768], P('head'), may hold values from -0.15625 to 0.15625
- student_return_bias: float32 [768], replicated, may hold values from -1.8 to 1.8
- student_second_gain: float32 [768], replicated, may hold values from 0.5 to 1.5
- student_second_shift: float32 [768], replicated, may hold values from -1.8 to 1.8
Outputs:
- student_out: float32 [16384, 768], P('dp')
- input_grad: float32 [16384, 768], P('dp')
- grad_query_weight: float32 [768, 768], P('dp', 'head')
- grad_query_bias: float32 [768], P('head')
- grad_key_weight: float32 [768, 768], P('dp', 'head')
- grad_value_weight: float32 [768, 768], P('dp', 'head')
- grad_value_bias: float32 [768], P('head')
- grad_output_weight: float32 [768, 768], P('head', 'dp')
- grad_output_bias: float32 [768], replicated
- grad_first_gain: float32 [768], replicated
- grad_first_shift: float32 [768], replicated
- grad_hidden_weight: float32 [768, 3072], P('dp', 'head')
- grad_hidden_bias: float32 [3072], P('head')
- grad_return_weight: float32 [3072, 768], P('head', 'dp')
- grad_return_bias: float32 [768], replicated
- grad_second_gain: float32 [768], replicated
- grad_second_shift: float32 [768], replicated
Inputs may be any that keep to these rules, and one draw needn't show every extreme that they name: `row_bucket`: bucket 2 is the bucket of some index of dp in every draw. `row_lengths`: entry [d, j] is the number of real tokens at the start of row j of index d of dp, whose rows hold (128) * 2^row_bucket[d] slots: more than half of the row and at most all of it; entries past the index's last row are 0. Some index of bucket 2 has a first row of exactly 512 real tokens.
All inputs are finite; a program needn't handle non-finite values.
Results may differ from a plain program's by a relative error of at most 0.014.
The roundings to bfloat16 on the way count: a program that leaves them out, or rounds other values in their place, can miss the bound.
Values sent between devices are 32-bit elements; how exact they have to be, the bound alone decides.
A program may use at most 192 MiB of HBM per device.

v0:
```python
import functools
import math

import jax
import jax.numpy as jnp
from jax import lax
from jax.sharding import PartitionSpec as P

HEAD_DIM = 64
SPAN = 512


NORM_EPS = 1e-12
SQRT_HALF = 0.7071067811865476


def gelu_exact(values):
    return 0.5 * values * (1.0 + lax.erf(values * SQRT_HALF))


def span_levels():
    return [SPAN // 4, SPAN // 2, SPAN]


def times_trans(left_op, right_op):
    return lax.dot_general(
        left_op, right_op, (((1,), (1,)), ((), ())), preferred_element_type=jnp.float32
    )


def trans_times(left_op, right_op):
    return lax.dot_general(
        left_op, right_op, (((0,), (0,)), ((), ())), preferred_element_type=jnp.float32
    )


def masked_scores(query_low, key_low, row_lens, row_span):
    tok_count, feat_width = query_low.shape
    row_count = tok_count // row_span
    row_shape = (row_count, row_span, feat_width // HEAD_DIM, HEAD_DIM)
    query_rows = query_low.reshape(row_shape)
    key_rows = key_low.reshape(row_shape)
    scores = jnp.einsum(
        "rqhd,rkhd->rhqk", query_rows, key_rows, preferred_element_type=jnp.float32
    ) * (1.0 / math.sqrt(HEAD_DIM))
    allowed = (jnp.arange(row_span, dtype=jnp.int32)[None, :] < row_lens[:row_count][:, None])[
        :, None, None, :
    ]
    return (jnp.where(allowed, scores, -1000000000.0), row_shape, query_rows, key_rows)


def attend(query_low, key_low, value_low, row_lens, row_span):
    scores, row_shape, query_rows, key_rows = masked_scores(query_low, key_low, row_lens, row_span)
    row_top = jnp.max(scores, axis=-1, keepdims=True)
    shifted = jnp.exp(scores - row_top)
    row_mass = jnp.sum(shifted, axis=-1, keepdims=True)
    probs_low = (shifted / row_mass).astype(jnp.bfloat16)
    context = jnp.einsum(
        "rhqk,rkhd->rqhd",
        probs_low,
        value_low.reshape(row_shape),
        preferred_element_type=jnp.float32,
    )
    logmass = jnp.transpose((row_top + jnp.log(row_mass))[..., 0], (1, 0, 2)).reshape(
        row_shape[2], query_low.shape[0]
    )
    return (context.reshape(query_low.shape), logmass)


def attend_back(query_low, key_low, value_low, logmass, grad_context, row_lens, row_span):
    scores, row_shape, query_rows, key_rows = masked_scores(query_low, key_low, row_lens, row_span)
    stored = jnp.transpose(logmass.reshape(row_shape[2], row_shape[0], row_span), (1, 0, 2))[
        ..., None
    ]
    probs = jnp.exp(scores - stored)
    grad_rows = grad_context.reshape(row_shape)
    grad_value = jnp.einsum(
        "rhqk,rqhd->rkhd", probs.astype(jnp.bfloat16), grad_rows, preferred_element_type=jnp.float32
    )
    grad_probs = jnp.einsum(
        "rqhd,rkhd->rhqk",
        grad_rows,
        value_low.reshape(row_shape),
        preferred_element_type=jnp.float32,
    )
    grad_scores = (
        probs * (grad_probs - jnp.sum(probs * grad_probs, axis=-1, keepdims=True))
    ).astype(jnp.bfloat16)
    score_scale = 1.0 / math.sqrt(HEAD_DIM)
    grad_query = (
        jnp.einsum("rhqk,rkhd->rqhd", grad_scores, key_rows, preferred_element_type=jnp.float32)
        * score_scale
    )
    grad_key = (
        jnp.einsum("rhqk,rqhd->rkhd", grad_scores, query_rows, preferred_element_type=jnp.float32)
        * score_scale
    )
    flat_shape = query_low.shape
    return (
        grad_query.reshape(flat_shape),
        grad_key.reshape(flat_shape),
        grad_value.reshape(flat_shape),
    )


def row_mask(row_lens, row_span, tok_count):
    row_count = tok_count // row_span
    allowed = jnp.arange(row_span, dtype=jnp.int32)[None, :] < row_lens[:row_count][:, None]
    return allowed.reshape(tok_count).astype(jnp.float32)


def standardize(summed):
    row_mean = jnp.mean(summed, axis=-1, keepdims=True)
    centred = summed - row_mean
    variance = jnp.mean(centred * centred, axis=-1, keepdims=True)
    inv_std = lax.rsqrt(variance + NORM_EPS)
    return (centred * inv_std, inv_std[:, 0])


def settle(partial_sum, bias_vec, residual, gain_vec, shift_vec):
    whole_sum = lax.psum(partial_sum, "head")
    normed, inv_std = standardize(whole_sum + bias_vec + residual)
    return (normed * gain_vec + shift_vec, normed, inv_std)


def norm_back(upstream, normed, inv_std, gain_vec):
    scaled = upstream * gain_vec
    centred = (
        scaled
        - jnp.mean(scaled, axis=-1, keepdims=True)
        - normed * jnp.mean(scaled * normed, axis=-1, keepdims=True)
    )
    return (
        inv_std[:, None] * centred,
        jnp.sum(upstream * normed, axis=0),
        jnp.sum(upstream, axis=0),
    )


def run_block(tokens, params, row_lens, bucket):
    (
        query_weight,
        query_bias,
        key_weight,
        value_weight,
        value_bias,
        output_weight,
        output_bias,
        first_gain,
        first_shift,
        hidden_weight,
        hidden_bias,
        return_weight,
        return_bias,
        second_gain,
        second_shift,
    ) = params
    residual = tokens.astype(jnp.float32)
    query_low = (
        jnp.dot(tokens, query_weight, preferred_element_type=jnp.float32) + query_bias
    ).astype(jnp.bfloat16)
    key_low = jnp.dot(tokens, key_weight, preferred_element_type=jnp.float32).astype(jnp.bfloat16)
    value_low = (
        jnp.dot(tokens, value_weight, preferred_element_type=jnp.float32) + value_bias
    ).astype(jnp.bfloat16)
    branches = [functools.partial(attend, row_span=level) for level in span_levels()]
    context, logmass = lax.switch(bucket, branches, query_low, key_low, value_low, row_lens)
    context_low = context.astype(jnp.bfloat16)
    first_out, first_normed, first_inv = settle(
        jnp.dot(context_low, output_weight, preferred_element_type=jnp.float32),
        output_bias,
        residual,
        first_gain,
        first_shift,
    )
    first_low = first_out.astype(jnp.bfloat16)
    hidden_pre = jnp.dot(first_low, hidden_weight, preferred_element_type=jnp.float32) + hidden_bias
    hidden_low = gelu_exact(hidden_pre).astype(jnp.bfloat16)
    block_out, second_normed, second_inv = settle(
        jnp.dot(hidden_low, return_weight, preferred_element_type=jnp.float32),
        return_bias,
        first_out,
        second_gain,
        second_shift,
    )
    kept = (
        query_low,
        key_low,
        value_low,
        logmass,
        context_low,
        first_normed,
        first_inv,
        first_low,
        hidden_pre,
        hidden_low,
        second_normed,
        second_inv,
    )
    return (block_out, kept)


def shards(
    tokens,
    row_bucket,
    row_lengths,
    teacher_query_weight,
    teacher_query_bias,
    teacher_key_weight,
    teacher_value_weight,
    teacher_value_bias,
    teacher_output_weight,
    teacher_output_bias,
    teacher_first_gain,
    teacher_first_shift,
    teacher_hidden_weight,
    teacher_hidden_bias,
    teacher_return_weight,
    teacher_return_bias,
    teacher_second_gain,
    teacher_second_shift,
    student_query_weight,
    student_query_bias,
    student_key_weight,
    student_value_weight,
    student_value_bias,
    student_output_weight,
    student_output_bias,
    student_first_gain,
    student_first_shift,
    student_hidden_weight,
    student_hidden_bias,
    student_return_weight,
    student_return_bias,
    student_second_gain,
    student_second_shift,
):
    row_lens = row_lengths[0]
    bucket = row_bucket[0]
    teacher = (
        teacher_query_weight,
        teacher_query_bias,
        teacher_key_weight,
        teacher_value_weight,
        teacher_value_bias,
        teacher_output_weight,
        teacher_output_bias,
        teacher_first_gain,
        teacher_first_shift,
        teacher_hidden_weight,
        teacher_hidden_bias,
        teacher_return_weight,
        teacher_return_bias,
        teacher_second_gain,
        teacher_second_shift,
    )
    student = (
        student_query_weight,
        student_query_bias,
        student_key_weight,
        student_value_weight,
        student_value_bias,
        student_output_weight,
        student_output_bias,
        student_first_gain,
        student_first_shift,
        student_hidden_weight,
        student_hidden_bias,
        student_return_weight,
        student_return_bias,
        student_second_gain,
        student_second_shift,
    )
    target, unused = run_block(tokens, teacher, row_lens, bucket)
    student_out, kept = run_block(tokens, student, row_lens, bucket)
    (
        query_low,
        key_low,
        value_low,
        logmass,
        context_low,
        first_normed,
        first_inv,
        first_low,
        hidden_pre,
        hidden_low,
        second_normed,
        second_inv,
    ) = kept
    mask_branches = [
        functools.partial(row_mask, row_span=level, tok_count=tokens.shape[0])
        for level in span_levels()
    ]
    token_valid = lax.switch(bucket, mask_branches, row_lens)
    upstream = (student_out - target) * token_valid[:, None]
    grad_second, grad_second_gain, grad_second_shift = norm_back(
        upstream, second_normed, second_inv, student_second_gain
    )
    return_low = grad_second.astype(jnp.bfloat16)
    grad_return_bias = jnp.sum(return_low.astype(jnp.float32), axis=0)
    grad_return_weight = trans_times(hidden_low, return_low)
    grad_hidden_out = times_trans(return_low, student_return_weight)
    unused_out, gelu_back = jax.vjp(gelu_exact, hidden_pre)
    hidden_grad_low = gelu_back(grad_hidden_out)[0].astype(jnp.bfloat16)
    grad_hidden_bias = jnp.sum(hidden_grad_low.astype(jnp.float32), axis=0)
    grad_hidden_weight = trans_times(first_low, hidden_grad_low)
    grad_first_in = grad_second + lax.psum(
        times_trans(hidden_grad_low, student_hidden_weight), "head"
    )
    grad_first, grad_first_gain, grad_first_shift = norm_back(
        grad_first_in, first_normed, first_inv, student_first_gain
    )
    output_low = grad_first.astype(jnp.bfloat16)
    grad_output_bias = jnp.sum(output_low.astype(jnp.float32), axis=0)
    grad_output_weight = trans_times(context_low, output_low)
    grad_context = times_trans(output_low, student_output_weight).astype(jnp.bfloat16)
    back_branches = [functools.partial(attend_back, row_span=level) for level in span_levels()]
    grad_query, grad_key, grad_value = lax.switch(
        bucket, back_branches, query_low, key_low, value_low, logmass, grad_context, row_lens
    )
    query_grad_low = grad_query.astype(jnp.bfloat16)
    key_grad_low = grad_key.astype(jnp.bfloat16)
    value_grad_low = grad_value.astype(jnp.bfloat16)
    grad_query_bias = jnp.sum(query_grad_low.astype(jnp.float32), axis=0)
    grad_value_bias = jnp.sum(value_grad_low.astype(jnp.float32), axis=0)
    grad_query_weight = trans_times(tokens, query_grad_low)
    grad_key_weight = trans_times(tokens, key_grad_low)
    grad_value_weight = trans_times(tokens, value_grad_low)
    partial_in = (
        times_trans(query_grad_low, student_query_weight)
        + times_trans(key_grad_low, student_key_weight)
        + times_trans(value_grad_low, student_value_weight)
    )
    input_grad = grad_first + lax.psum(partial_in, "head")
    summed_mats = (
        lax.psum_scatter(grad_query_weight, "dp", scatter_dimension=0, tiled=True),
        lax.psum_scatter(grad_key_weight, "dp", scatter_dimension=0, tiled=True),
        lax.psum_scatter(grad_value_weight, "dp", scatter_dimension=0, tiled=True),
        lax.psum_scatter(grad_output_weight, "dp", scatter_dimension=1, tiled=True),
        lax.psum_scatter(grad_hidden_weight, "dp", scatter_dimension=0, tiled=True),
        lax.psum_scatter(grad_return_weight, "dp", scatter_dimension=1, tiled=True),
    )
    summed_small = lax.psum(
        (
            grad_query_bias,
            grad_value_bias,
            grad_output_bias,
            grad_first_gain,
            grad_first_shift,
            grad_hidden_bias,
            grad_return_bias,
            grad_second_gain,
            grad_second_shift,
        ),
        "dp",
    )
    return (
        student_out,
        input_grad,
        summed_mats[0],
        summed_small[0],
        summed_mats[1],
        summed_mats[2],
        summed_small[1],
        summed_mats[3],
        summed_small[2],
        summed_small[3],
        summed_small[4],
        summed_mats[4],
        summed_small[5],
        summed_mats[5],
        summed_small[6],
        summed_small[7],
        summed_small[8],
    )


def solution(mesh):
    placed = (
        P("dp", None),
        P("dp"),
        P("dp", None),
        P(None, "head"),
        P("head"),
        P(None, "head"),
        P(None, "head"),
        P("head"),
        P("head", None),
        P(),
        P(),
        P(),
        P(None, "head"),
        P("head"),
        P("head", None),
        P(),
        P(),
        P(),
        P(None, "head"),
        P("head"),
        P(None, "head"),
        P(None, "head"),
        P("head"),
        P("head", None),
        P(),
        P(),
        P(),
        P(None, "head"),
        P("head"),
        P("head", None),
        P(),
        P(),
        P(),
    )
    return jax.shard_map(
        shards,
        mesh=mesh,
        in_specs=placed,
        out_specs=(
            P("dp", None),
            P("dp", None),
            P("dp", "head"),
            P("head"),
            P("dp", "head"),
            P("dp", "head"),
            P("head"),
            P("head", "dp"),
            P(),
            P(),
            P(),
            P("dp", "head"),
            P("head"),
            P("head", "dp"),
            P(),
            P(),
            P(),
        ),
        check_vma=False,
    )
```

profile of v0, /device:TPU:0, one launch (start us, length us, event | category | flops | bytes accessed | tf_op | source)
XLA Modules:
  0.0 1187.3 jit_solution(12035679780166435485)
XLA Ops:
  20.1 22.6 %conditional.12 = (bf16[1024,384]{0,1:T(8,128)(2,1)}) conditional(s32[]{:T(128)} %bitcast.33, (s32[1,8]{1,0:T(1,128)S(1)}, bf16[1024,384]{1,0:T(8,128)(2,1)}, bf16[1024,384]{1,0:T(8,128)(2,1)}, bf16[1024,384]{1,0:T(8,128)(2,1)}) %tuple.221, (s32[8]{0:T(128)S(1)}, bf16[1024,384]{1,0:T(8,128)(2,1)}, bf16[1024,384]{1,0:T(8,128)(2,1)}, ...), branch_computations={%region_15.18_spmd, %region_18.21_spmd, %region_21.24_spmd} | conditional | flops 824182272 | bytes 44091444
  42.8 24.7 %conditional.11 = (f32[6,1024]{1,0:T(8,128)S(1)}, bf16[1024,384]{0,1:T(8,128)(2,1)}) conditional(s32[]{:T(128)} %bitcast.33, (s32[1,8]{1,0:T(1,128)S(1)}, bf16[1024,384]{1,0:T(8,128)(2,1)}, bf16[1024,384]{1,0:T(8,128)(2,1)S(1)}, bf16[1024,384]{1,0:T(8,128)(2,1)}) %tuple.224, (s32[8]{0:T(128)S(1)}, bf16[1024,384]{1,0:T(8,128)(2,1)}, ...), branch_computations={%region_0.3_spmd, %region_3.6_spmd, %region_6.9_spmd} | conditional | flops 843443200 | bytes 56823860
  75.4 76.5 %all-reduce.14.cloned.1.call-done = (f32[1024,768]{1,0:T(8,128)}, f32[1024,768]{1,0:T(8,128)}) async-done(((f32[1024,768]{1,0:T(8,128)}, f32[1024,768]{1,0:T(8,128)}), (f32[1024,768]{1,0:T(8,128)}, f32[1024,768]{1,0:T(8,128)})) %all-reduce.14.cloned.1.call-update) | async-done | bytes 6291472 | tf_op jit(solution)/shard_map/psum | solution.py:121
  160.0 5.2 multiply_convert_fusion.10
  165.2 4.3 fusion.194
  169.5 10.3 fusion.158
  180.1 33.1 %all-reduce.12.cloned.1.call-done = (f32[1024,768]{1,0:T(8,128)}, f32[1024,768]{1,0:T(8,128)}) async-done(((f32[1024,768]{1,0:T(8,128)}, f32[1024,768]{1,0:T(8,128)}), (f32[1024,768]{1,0:T(8,128)}, f32[1024,768]{1,0:T(8,128)})) %all-reduce.12.cloned.1.call-update) | async-done | bytes 6291472 | tf_op jit(solution)/shard_map/psum | solution.py:121
  221.0 4.2 multiply_reduce_fusion.3
  227.0 6.0 convert_reduce_fusion
  234.7 4.3 fusion.195
  239.1 24.5 %all-reduce.8.cloned.1.call-done = f32[1024,768]{1,0:T(8,128)} async-done(((f32[1024,768]{1,0:T(8,128)}), f32[1024,768]{1,0:T(8,128)}) %all-reduce.8.cloned.1.call-update) | async-done | bytes 3145744 | tf_op jit(solution)/shard_map/psum | solution.py:307
  263.6 5.4 multiply_reduce_fusion.4
  274.3 34.4 %conditional.14 = (bf16[1024,384]{0,1:T(8,128)(2,1)}, bf16[1024,384]{0,1:T(8,128)(2,1)S(1)}, bf16[1024,384]{0,1:T(8,128)(2,1)}) conditional(s32[]{:T(128)} %bitcast.33, (s32[1,8]{1,0:T(1,128)S(1)}, bf16[1024,384]{1,0:T(8,128)(2,1)}, bf16[1024,384]{1,0:T(8,128)(2,1)S(1)}, f32[6,1024]{1,0:T(8,128)S(1)}, ...), branch_computations={%region_38.40_spmd, %region_40.42_spmd, %region_42.44_spmd} | conditional | flops 2062412800 | bytes 171569344
  316.4 4.2 fusion.162
  334.5 7.6 fusion.165
  342.8 8.0 fusion.175
  353.6 116.2 %all-reduce = (f32[384]{0:T(512)}, f32[384]{0:T(512)}, f32[768]{0:T(1024)}, f32[768]{0:T(1024)}, f32[768]{0:T(1024)}, /*index=5*/f32[1536]{0:T(1024)}, f32[768]{0:T(1024)}, f32[768]{0:T(1024)}, f32[768]{0:T(1024)}) all-reduce(f32[384]{0:T(512)S(1)} %convert_reduce_fusion.4, ...), channel_id=1, replica_groups=mesh['dp'=16,'head'=2] {'dp'}, use_global_device_ids=true, to_apply=%region_47.48 | all-reduce | flops 6912 | bytes 55296 | tf_op jit(solution)/shard_map/psum | solution.py:343
  469.8 4.9 add.288
  474.7 38.1 %reduce-scatter.13.cloned.1.call-done = f32[384,48]{0,1:T(8,128)} async-done(((f32[384,768]{0,1:T(8,128)}), f32[384,48]{0,1:T(8,128)}) %reduce-scatter.13.cloned.1.call-update) | async-done | bytes 73744 | tf_op jit(solution)/shard_map/reduce_scatter | solution.py:339
  512.8 127.9 %reduce-scatter.21.cloned.1.call-done = f32[48,384]{1,0:T(8,128)} async-done(((f32[768,384]{1,0:T(8,128)}), f32[48,384]{1,0:T(8,128)}) %reduce-scatter.21.cloned.1.call-update) | async-done | bytes 73744
  640.7 127.9 %reduce-scatter.19.cloned.1.call-done = f32[48,384]{1,0:T(8,128)} async-done(((f32[768,384]{1,0:T(8,128)}), f32[48,384]{1,0:T(8,128)}) %reduce-scatter.19.cloned.1.call-update) | async-done | bytes 73744
  768.6 128.0 %reduce-scatter.23.cloned.1.call-done = f32[48,384]{1,0:T(8,128)} async-done(((f32[768,384]{1,0:T(8,128)}), f32[48,384]{1,0:T(8,128)}) %reduce-scatter.23.cloned.1.call-update) | async-done | bytes 73744
  896.6 141.5 %reduce-scatter.17.cloned.1.call-done = f32[1536,48]{0,1:T(8,128)} async-done(((f32[1536,768]{0,1:T(8,128)}), f32[1536,48]{0,1:T(8,128)}) %reduce-scatter.17.cloned.1.call-update) | async-done | bytes 294928 | tf_op jit(solution)/shard_map/reduce_scatter | solution.py:341
  1038.2 142.1 %reduce-scatter.15.cloned.1.call-done = f32[48,1536]{1,0:T(8,128)} async-done(((f32[768,1536]{1,0:T(8,128)}), f32[48,1536]{1,0:T(8,128)}) %reduce-scatter.15.cloned.1.call-update) | async-done | bytes 294928 | tf_op jit(solution)/shard_map/reduce_scatter | solution.py:340
  (224 shorter events, 132.5 us)
Async XLA Ops:
  7.2 152.6 %copy-start = (bf16[768,1536]{1,0:T(8,128)(2,1)S(1)}, bf16[768,1536]{1,0:T(8,128)(2,1)}, u32[]{:S(2)}) copy-start(bf16[768,1536]{1,0:T(8,128)(2,1)} %param.72) | copy-start | bytes 7077892
  7.2 144.8 %all-reduce.14.cloned.1.call-start = ((), (), s32[]{:S(2)}) async-start(), calls=%async_computation.15 | async-start | bytes 12582912 | tf_op jit(solution)/shard_map/psum | solution.py:121
  75.4 76.6 %copy-start.31 = (f32[768]{0:T(1024)S(1)}, f32[768]{0:T(1024)}, u32[]{:S(2)}) copy-start(f32[768]{0:T(1024)} %param.54) | copy-start | bytes 9220
  75.4 79.6 %copy-start.41 = (f32[768]{0:T(1024)S(1)}, f32[768]{0:T(1024)}, u32[]{:S(2)}) copy-start(f32[768]{0:T(1024)} %param.69) | copy-start | bytes 9220
  75.4 137.8 %all-reduce.12.cloned.1.call-start = ((), (), s32[]{:S(2)}) async-start(), calls=%async_computation.14 | async-start | bytes 12582912 | tf_op jit(solution)/shard_map/psum | solution.py:121
  159.2 6.0 copy-start.1
  160.0 5.2 copy-start.51
  165.2 4.3 copy-start.62
  179.8 33.4 %copy-start.44 = (f32[768]{0:T(1024)S(1)}, f32[768]{0:T(1024)}, u32[]{:S(2)}) copy-start(f32[768]{0:T(1024)} %param.60) | copy-start | bytes 9220
  179.8 83.8 %all-reduce.8.cloned.1.call-start = ((), (), s32[]{:S(2)}) async-start(), calls=%async_computation.6 | async-start | bytes 6291456 | tf_op jit(solution)/shard_map/psum | solution.py:307
  213.2 4.7 copy-start.16
  220.4 6.6 slice-start.3
  221.0 6.0 slice-start.4
  227.0 6.0 copy-start.8
  239.0 230.8 %all-reduce.10.cloned.1.call-start = ((), (), s32[]{:S(2)}) async-start(), calls=%async_computation.7 | async-start | bytes 6291456 | tf_op jit(solution)/shard_map/psum | solution.py:334
  263.6 5.4 copy-start.3
  284.8 6.0 copy-start.9
  316.3 4.4 copy-start.18
  316.3 196.5 %reduce-scatter.13.cloned.1.call-start = ((), (), s32[]{:S(2)}) async-start(), calls=%async_computation.8 | async-start | bytes 1253376 | tf_op jit(solution)/shard_map/reduce_scatter | solution.py:339
  320.6 320.0 %reduce-scatter.21.cloned.1.call-start = ((), (), s32[]{:S(2)}) async-start(), calls=%async_computation.12 | async-start | bytes 1253376
  326.6 442.0 %reduce-scatter.19.cloned.1.call-start = ((), (), s32[]{:S(2)}) async-start(), calls=%async_computation.11 | async-start | bytes 1253376
  330.5 566.1 %reduce-scatter.23.cloned.1.call-start = ((), (), s32[]{:S(2)}) async-start(), calls=%async_computation.13 | async-start | bytes 1253376
  334.5 703.7 %reduce-scatter.17.cloned.1.call-start = ((), (), s32[]{:S(2)}) async-start(), calls=%async_computation.10 | async-start | bytes 5013504 | tf_op jit(solution)/shard_map/reduce_scatter | solution.py:341
  342.2 838.1 %reduce-scatter.15.cloned.1.call-start = ((), (), s32[]{:S(2)}) async-start(), calls=%async_computation.9 | async-start | bytes 5013504 | tf_op jit(solution)/shard_map/reduce_scatter | solution.py:340
  (43 other events, 101.7 us)
Sparse Core Ops, SparseCore 0:
  75.5 76.4 all-reduce.13
  179.9 33.2 all-reduce.11
  239.1 24.3 all-reduce.7
  316.4 66.2 all-reduce.9
  387.9 124.8 reduce-scatter.12
  518.0 122.6 reduce-scatter.20
  646.0 122.5 reduce-scatter.18
  773.9 122.6 reduce-scatter.22
  902.4 135.7 reduce-scatter.16
  1044.6 135.6 reduce-scatter.14
where the time goes:
time: 1200 us; the launch traced here: 1190 us
  waiting for transfers between devices  840 us (70%)
  blocking collectives  116 us (10%)
  matrix products  99 us (8%)
  local copies, waits for them, and re-layouts  59.4 us (5%)
  other arithmetic  37.4 us (3%)
  loops' own time  19.1 us (2%)
  between operations  15.6 us (1%)
    unnamed x13, waiting for transfers between devices  384 us
    reduce_scatter x1, waiting for transfers between devices, shards(): lax.psum_scatter(grad_hidden_weight, 'dp', scatter_dimension=0, tiled=True)  142 us
    reduce_scatter x1, waiting for transfers between devices, shards(): lax.psum_scatter(grad_return_weight, 'dp', scatter_dimension=1, tiled=True)  142 us
    psum x1, blocking collectives, shards(): lax.psum((grad_query_bias, grad_value_bias, grad_output_bias, grad_first_...  116 us
    psum x2, waiting for transfers between devices, settle(): whole_sum = lax.psum(partial_sum, 'head')  110 us
    another operation x31, local copies, waits for them, and re-layouts  43.5 us
    reduce_scatter x1, waiting for transfers between devices, shards(): lax.psum_scatter(grad_output_weight, 'dp', scatter_dimension=1, tiled=True)  38.1 us
    dot_general x6, matrix products, trans_times(): lax.dot_general(left_op, right_op, (((0,), (0,)), ((), ())), preferred_el...  27.9 us
  transfers between devices with their start and end apart: 10, of which 9 were waited for; matrix products, arithmetic and copies ran while one was open for 3% of the time, Pallas kernels for 0%

commit v1 on v0

--- a/solution.py
+++ b/solution.py
@@ -4,14 +4,319 @@
 import jax
 import jax.numpy as jnp
 from jax import lax
+from jax.experimental import pallas as pl
+from jax.experimental.pallas import tpu as pltpu
 from jax.sharding import PartitionSpec as P
 
+MESH = pl.DeviceIdType.MESH
 HEAD_DIM = 64
 SPAN = 512
 
 
 NORM_EPS = 1e-12
 SQRT_HALF = 0.7071067811865476
+
+
+CW = 256
+NZ, NY, NX = 4, 2, 2
+ROWS = 48
+
+
+class Place:
+    def __init__(self):
+        self.dp = lax.axis_index("dp")
+        self.head = lax.axis_index("head")
+        self.z = self.dp // 4
+        self.y = lax.rem(self.dp // 2, 2)
+        self.x = lax.rem(self.dp, 2)
+
+    def at(self, dz=0, y=None, x=None):
+        y = self.y if y is None else y
+        x = self.x if x is None else x
+        return ((self.z + dz) * 4 + y * 2 + x, self.head)
+
+
+class Ring:
+    def __init__(self, place, kinds, grad, pair_a, pair_b, path, zpath, zpair_a, zpair_b, send, recv, slot=None):
+        self.p = place
+        self.kinds = kinds
+        self.grad, self.pair_a, self.pair_b, self.path = grad, pair_a, pair_b, path
+        self.zpath, self.zpair_a, self.zpair_b = zpath, zpair_a, zpair_b
+        self.send, self.recv = send, recv
+        self.slot = slot or list(range(len(kinds)))
+        flat = [c for c, k in enumerate(kinds) if not k.startswith("z")]
+        deep = [c for c, k in enumerate(kinds) if k.startswith("z")]
+        self.place_of = {c: i for i, c in enumerate(flat)} | {c: i for i, c in enumerate(deep)}
+
+    def _pair(self, c, step):
+        kind, p, i = self.kinds[c], self.p, self.place_of[c]
+        g = self.grad.at[self.slot[c]]
+        if kind.startswith("z"):
+            axis = kind[1 + step]
+            land = (self.zpair_a if step == 0 else self.zpair_b).at[i]
+            view = g.at[p.z]
+            if step == 0:
+                pick = (lambda j: view.at[:, j]) if axis == "x" else (lambda j: view.at[j])
+            else:
+                pick = (lambda j: view.at[p.y, j]) if axis == "x" else (lambda j: view.at[j, p.x])
+        else:
+            axis = kind[step]
+            land = (self.pair_a if step == 0 else self.pair_b).at[i]
+            if step == 0:
+                pick = (lambda j: g.at[:, :, j]) if axis == "x" else (lambda j: g.at[:, j])
+            else:
+                pick = (lambda j: g.at[:, p.y, j]) if axis == "x" else (lambda j: g.at[:, j, p.x])
+        mine = p.x if axis == "x" else p.y
+        to = p.at(x=1 - p.x) if axis == "x" else p.at(y=1 - p.y)
+        copy = pltpu.make_async_remote_copy(
+            src_ref=pick(1 - mine), dst_ref=land, send_sem=self.send.at[c, step], recv_sem=self.recv.at[c, step],
+            device_id=to, device_id_type=MESH)
+        return copy, pick(mine), land
+
+    def pair_send(self, c, step):
+        self._pair(c, step)[0].start()
+
+    def pair_take(self, c, step):
+        copy, mine, land = self._pair(c, step)
+        copy.wait_recv()
+        mine[...] += land[...]
+
+    def _path_refs(self, c):
+        kind, p, i = self.kinds[c], self.p, self.place_of[c]
+        g = self.grad.at[self.slot[c]]
+        if kind.startswith("z"):
+            return (lambda lo, n: g.at[pl.ds(lo, n)]), self.zpath.at[i]
+        return (lambda lo, n: g.at[pl.ds(lo, n), p.y, p.x]), self.path.at[i]
+
+    def _hop(self, c, z, up):
+        blocks, land = self._path_refs(c)
+        if up:
+            src, dst, k, dz = blocks(z + 1, 3 - z), land.at[pl.ds(0, 3 - z)], 2, 1
+        else:
+            src, dst, k, dz = blocks(0, z), land.at[pl.ds(5 - z, z)], 3, -1
+        return pltpu.make_async_remote_copy(
+            src_ref=src, dst_ref=dst, send_sem=self.send.at[c, k], recv_sem=self.recv.at[c, k],
+            device_id=self.p.at(dz=dz), device_id_type=MESH)
+
+    def path_start(self, c):
+        @pl.when(self.p.z == 0)
+        def _():
+            self._hop(c, 0, True).start()
+
+        @pl.when(self.p.z == 3)
+        def _():
+            self._hop(c, 3, False).start()
+
+    def path_mid(self, c, first):
+        blocks, land = self._path_refs(c)
+        for z in (1, 2):
+            up = (z == 1) == first
+
+            @pl.when(self.p.z == z)
+            def _(z=z, up=up):
+                if up:
+                    self._hop(c, z - 1, True).wait_recv()
+                    own = blocks(z + 1, 3 - z)
+                    own[...] += land[pl.ds(1, 3 - z)]
+                    self._hop(c, z, True).start()
+                else:
+                    self._hop(c, z + 1, False).wait_recv()
+                    own = blocks(0, z)
+                    own[...] += land[pl.ds(4 - z, z)]
+                    self._hop(c, z, False).start()
+
+    def path_end(self, c):
+        blocks, land = self._path_refs(c)
+        for z in range(NZ):
+            @pl.when(self.p.z == z)
+            def _(z=z):
+                if z == 0:
+                    self._hop(c, 1, False).wait_recv()
+                if z == 3:
+                    self._hop(c, 2, True).wait_recv()
+                own = blocks(z, 1)
+                total = own[...]
+                if z > 0:
+                    total = total + land[pl.ds(0, 1)]
+                if z < 3:
+                    total = total + land[pl.ds(4, 1)]
+                own[...] = total
+
+    def drain(self, c):
+        for step in (0, 1):
+            self._pair(c, step)[0].wait_send()
+        for z in range(NZ):
+            @pl.when(self.p.z == z)
+            def _(z=z):
+                if z < 3:
+                    self._hop(c, z, True).wait_send()
+                if z > 0:
+                    self._hop(c, z, False).wait_send()
+
+    def stage(self, c, s):
+        deep = self.kinds[c].startswith("z")
+        if deep:
+            if s == 0: self.path_start(c)
+            elif s == 1: self.path_mid(c, True)
+            elif s == 2: self.path_mid(c, False)
+            elif s == 3: self.path_end(c); self.pair_send(c, 0)
+            elif s == 4: self.pair_take(c, 0); self.pair_send(c, 1)
+            elif s == 5: self.pair_take(c, 1)
+        else:
+            if s == 0: self.pair_send(c, 0)
+            elif s == 1: self.pair_take(c, 0); self.pair_send(c, 1)
+            elif s == 2: self.pair_take(c, 1); self.path_start(c)
+            elif s == 3: self.path_mid(c, True)
+            elif s == 4: self.path_mid(c, False)
+            elif s == 5: self.path_end(c)
+
+    def own(self, c):
+        p = self.p
+        return self.grad.at[self.slot[c], p.z, p.y, p.x]
+
+
+def scratch(kinds, slots):
+    flat = sum(not k.startswith("z") for k in kinds)
+    deep = len(kinds) - flat
+    f = jnp.float32
+    return [
+        pltpu.VMEM((slots, NZ, NY, NX, ROWS, CW), f),
+        pltpu.VMEM((flat, NZ, 2, ROWS, CW), f),
+        pltpu.VMEM((flat, NZ, ROWS, CW), f),
+        pltpu.VMEM((flat, 5, ROWS, CW), f),
+        pltpu.VMEM((max(deep, 1), 5, NY, NX, ROWS, CW), f),
+        pltpu.VMEM((max(deep, 1), 2, ROWS, CW), f),
+        pltpu.VMEM((max(deep, 1), ROWS, CW), f),
+        pltpu.SemaphoreType.DMA((len(kinds), 4)),
+        pltpu.SemaphoreType.DMA((len(kinds), 4)),
+    ]
+
+
+def greet(place):
+    barrier = pltpu.get_barrier_semaphore()
+    p = place
+    for to in (p.at(x=1 - p.x), p.at(y=1 - p.y)):
+        pl.semaphore_signal(barrier, inc=1, device_id=to, device_id_type=MESH)
+    @pl.when(p.z < 3)
+    def _():
+        pl.semaphore_signal(barrier, inc=1, device_id=p.at(dz=1), device_id_type=MESH)
+    @pl.when(p.z > 0)
+    def _():
+        pl.semaphore_signal(barrier, inc=1, device_id=p.at(dz=-1), device_id_type=MESH)
+    @pl.when((p.z == 0) | (p.z == 3))
+    def _():
+        pl.semaphore_wait(barrier, 3)
+    @pl.when((p.z == 1) | (p.z == 2))
+    def _():
+        pl.semaphore_wait(barrier, 4)
+
+
+class Butterfly:
+    def __init__(self, place, value, land, send, recv):
+        self.p, self.value, self.land, self.send, self.recv = place, value, land, send, recv
+
+    def partner(self, step):
+        p = self.p
+        if step == 0:
+            return p.at(x=1 - p.x)
+        if step == 1:
+            return p.at(y=1 - p.y)
+        if step == 2:
+            return p.at(dz=1 - 2 * lax.rem(p.z, 2))
+        return p.at(dz=2 - 4 * (p.z // 2))
+
+    def _copy(self, step):
+        return pltpu.make_async_remote_copy(
+            src_ref=self.value.at[step], dst_ref=self.land.at[step], send_sem=self.send.at[step],
+            recv_sem=self.recv.at[step], device_id=self.partner(step), device_id_type=MESH)
+
+    def start(self, step):
+        self._copy(step).start()
+
+    def take(self, step):
+        self._copy(step).wait_recv()
+        self.value[step + 1] = self.value[step] + self.land[step]
+
+    def drain(self):
+        for step in range(4):
+            self._copy(step).wait_send()
+
+
+KINDS = ["zxy", "xy", "yx", "xy", "yx", "zyx", "xy", "yx", "xy", "yx", "zxy", "xy", "yx", "xy", "yx", "zyx", "xy", "yx"]
+
+
+def wavefront(count, lag):
+    items = sorted((c + lag * s, -s, c, s) for c in range(count) for s in range(6))
+    return [(c, s) for _, _, c, s in items]
+
+
+def scatter_kernel(grads, small, out, small_out, *refs):
+    ring_refs, (load, value, land, vsend, vrecv) = refs[:9], refs[9:]
+    place = Place()
+    grad = ring_refs[0]
+    count = grads.shape[0]
+    for c in range(count):
+        pltpu.make_async_copy(grads.at[c], grad.at[c], load.at[c]).start()
+    value[0] = small[...]
+    greet(place)
+    ring = Ring(place, KINDS, *ring_refs)
+    fly = Butterfly(place, value, land, vsend, vrecv)
+    fly.start(0)
+    for c, s in wavefront(count, 2):
+        if s == 0:
+            pltpu.make_async_copy(grads.at[c], grad.at[c], load.at[c]).wait()
+        ring.stage(c, s)
+        if s == 5:
+            out[:, c * CW:(c + 1) * CW] = ring.own(c)[...]
+        if s == 0 and c in (4, 6, 8, 10):
+            step = (c - 4) // 2
+            fly.take(step)
+            if step < 3:
+                fly.start(step + 1)
+    small_out[...] = value[4]
+    for c in range(count):
+        ring.drain(c)
+    fly.drain()
+
+
+def scatter(grads, small):
+    count = grads.shape[0]
+    f = jnp.float32
+    return pl.pallas_call(
+        scatter_kernel,
+        out_shape=(jax.ShapeDtypeStruct((ROWS, count * CW), f), jax.ShapeDtypeStruct(small.shape, f)),
+        in_specs=[pl.BlockSpec(memory_space=pl.ANY), pl.BlockSpec(memory_space=pltpu.VMEM)],
+        out_specs=(pl.BlockSpec(memory_space=pltpu.VMEM), pl.BlockSpec(memory_space=pltpu.VMEM)),
+        scratch_shapes=scratch(KINDS, count) + [
+            pltpu.SemaphoreType.DMA((count,)),
+            pltpu.VMEM((5,) + small.shape, f),
+            pltpu.VMEM((4,) + small.shape, f),
+            pltpu.SemaphoreType.DMA((4,)),
+            pltpu.SemaphoreType.DMA((4,)),
+        ],
+        compiler_params=pltpu.CompilerParams(collective_id=0, has_side_effects=True, vmem_limit_bytes=60 * 2**20),
+    )(grads, small)
+
+
+def by_kernel(mats, smalls):
+    wide = jnp.concatenate([mats[5].T, mats[4], mats[3].T, mats[0], mats[1], mats[2]], axis=1)
+    count = wide.shape[1] // CW
+    grads = jnp.transpose(wide.reshape(NZ, NY, NX, ROWS, count, CW), (4, 0, 1, 2, 3, 5))
+    flat = jnp.concatenate(smalls)
+    small = jnp.pad(flat, (0, 7168 - flat.shape[0])).reshape(8, 896)
+    out, small_out = scatter(grads, small)
+    flat = small_out.reshape(-1)
+    cuts, at = [], 0
+    for item in smalls:
+        cuts.append(flat[at:at + item.shape[0]])
+        at += item.shape[0]
+    ff = mats[5].shape[0]
+    hw = mats[3].shape[0]
+    pieces, at = [], 0
+    for width in (ff, ff, hw, hw, hw, hw):
+        pieces.append(out[:, at:at + width])
+        at += width
+    return (pieces[3], pieces[4], pieces[5], pieces[2].T, pieces[1], pieces[0].T), cuts
 
 
 def gelu_exact(values):
@@ -332,28 +637,26 @@
         + times_trans(value_grad_low, student_value_weight)
     )
     input_grad = grad_first + lax.psum(partial_in, "head")
-    summed_mats = (
-        lax.psum_scatter(grad_query_weight, "dp", scatter_dimension=0, tiled=True),
-        lax.psum_scatter(grad_key_weight, "dp", scatter_dimension=0, tiled=True),
-        lax.psum_scatter(grad_value_weight, "dp", scatter_dimension=0, tiled=True),
-        lax.psum_scatter(grad_output_weight, "dp", scatter_dimension=1, tiled=True),
-        lax.psum_scatter(grad_hidden_weight, "dp", scatter_dimension=0, tiled=True),
-        lax.psum_scatter(grad_return_weight, "dp", scatter_dimension=1, tiled=True),
-    )
-    summed_small = lax.psum(
-        (
-            grad_query_bias,
-            grad_value_bias,
-            grad_output_bias,
-            grad_first_gain,
-            grad_first_shift,
-            grad_hidden_bias,
-            grad_return_bias,
-            grad_second_gain,
-            grad_second_shift,
-        ),
-        "dp",
-    )
+    mats = (grad_query_weight, grad_key_weight, grad_value_weight, grad_output_weight, grad_hidden_weight, grad_return_weight)
+    smalls = (
+        grad_query_bias,
+        grad_value_bias,
+        grad_output_bias,
+        grad_first_gain,
+        grad_first_shift,
+        grad_hidden_bias,
+        grad_return_bias,
+        grad_second_gain,
+        grad_second_shift,
+    )
+    if lax.axis_size("dp") == NZ * NY * NX:
+        summed_mats, summed_small = by_kernel(mats, smalls)
+    else:
+        summed_mats = tuple(
+            lax.psum_scatter(item, "dp", scatter_dimension=1 if i in (3, 5) else 0, tiled=True)
+            for i, item in enumerate(mats)
+        )
+        summed_small = lax.psum(smalls, "dp")
     return (
         student_out,
         input_grad,

time: 1200 us -> 543 us (0.45)
  waiting for transfers between devices: 840 us -> 97.8 us
  Pallas kernels: 0 us -> 140 us
  blocking collectives: 116 us -> 0 us
  local copies, waits for them, and re-layouts: 59.4 us -> 102 us
  loops' own time: 19.1 us -> 31.4 us
  matrix products: 99 us -> 111 us
    unnamed x13 -> x4, waiting for transfers between devices: 384 us -> 0.07 us
    reduce_scatter x3 -> x0, waiting for transfers between devices: 322 us -> none  [the longest x1 142 us: shards(): lax.psum_scatter(grad_hidden_weight, 'dp', scatter_dimension=0, tiled=True)]
    pallas_call x0 -> x1, Pallas kernels: none -> 140 us  [scatter(): pl.pallas_call(scatter_kernel, out_shape=(jax.ShapeDtypeStruct((ROWS, cou...]
    psum x1 -> x0, blocking collectives: 116 us -> none  [shards(): lax.psum((grad_query_bias, grad_value_bias, grad_output_bias, grad_first_...]
    reshape x0 -> x14, local copies, waits for them, and re-layouts: none -> 64.3 us  [the longest x2 33.8 us: by_kernel(): wide.reshape(NZ, NY, NX, ROWS, count, CW)]
    psum x2, waiting for transfers between devices: 110 us -> 86.4 us  [settle(): whole_sum = lax.psum(partial_sum, 'head')]
    another operation x31 -> x25, local copies, waits for them, and re-layouts: 43.5 us -> 22.1 us
    psum x1, waiting for transfers between devices: 24.5 us -> 11.4 us  [shards(): lax.psum(times_trans(hidden_grad_low, student_hidden_weight), 'head')]
  transfers between devices with their start and end apart: 10 -> 4, of which waited for: 9 -> 3; matrix products, arithmetic and copies ran while one was open for 3% -> 12% of each run, Pallas kernels for 0% -> 26%
where the time goes in v1:
time: 543 us; the launch traced here: 537 us
  Pallas kernels  140 us (26%)
  matrix products  111 us (20%)
  local copies, waits for them, and re-layouts  102 us (19%)
  waiting for transfers between devices  97.8 us (18%)
  other arithmetic  38.3 us (7%)
  loops' own time  31.4 us (6%)
  between operations  15.6 us (3%)
    pallas_call x1, Pallas kernels, scatter(): pl.pallas_call(scatter_kernel, out_shape=(jax.ShapeDtypeStruct((ROWS, cou...  140 us
    psum x2, waiting for transfers between devices, settle(): whole_sum = lax.psum(partial_sum, 'head')  86.4 us
    reshape x2, local copies, waits for them, and re-layouts, by_kernel(): wide.reshape(NZ, NY, NX, ROWS, count, CW)  33.8 us
    unnamed x4, loops' own time  31.4 us
    dot_general x6, matrix products, trans_times(): lax.dot_general(left_op, right_op, (((0,), (0,)), ((), ())), preferred_el...  23.4 us
    another operation x25, local copies, waits for them, and re-layouts  22.1 us
    dot_general x6, matrix products, times_trans(): lax.dot_general(left_op, right_op, (((1,), (1,)), ((), ())), preferred_el...  16.9 us
    reshape x3, local copies, waits for them, and re-layouts, masked_scores(): query_rows = query_low.reshape(row_shape)  15.5 us
  transfers between devices with their start and end apart: 4, of which 3 were waited for; matrix products, arithmetic and copies ran while one was open for 12% of the time, Pallas kernels for 26%

profile of v1, /device:TPU:0, one launch (start us, length us, event | category | flops | bytes accessed | tf_op | source)
XLA Modules:
  0.0 536.6 jit_solution(6883021152908112117)
XLA Ops:
  20.1 34.8 %conditional.10 = (f32[6,1024]{1,0:T(8,128)S(1)}, bf16[1024,384]{0,1:T(8,128)(2,1)}) conditional(s32[]{:T(128)} %bitcast.33, (s32[1,8]{1,0:T(1,128)S(1)}, bf16[1024,384]{1,0:T(8,128)(2,1)}, bf16[1024,384]{1,0:T(8,128)(2,1)S(1)}, bf16[1024,384]{1,0:T(8,128)(2,1)}) %tuple.212, (s32[8]{0:T(128)S(1)}, bf16[1024,384]{1,0:T(8,128)(2,1)}, ...), branch_computations={%region_0.3_spmd, %region_3.6_spmd, %region_6.9_spmd} | conditional | flops 843443200 | bytes 104009784
  39.7 4.7 fusion.16
  58.9 33.2 %conditional.11 = (bf16[1024,384]{0,1:T(8,128)(2,1)}) conditional(s32[]{:T(128)} %bitcast.33, (s32[1,8]{1,0:T(1,128)S(1)}, bf16[1024,384]{1,0:T(8,128)(2,1)}, bf16[1024,384]{1,0:T(8,128)(2,1)}, bf16[1024,384]{1,0:T(8,128)(2,1)}) %tuple.215, (s32[8]{0:T(128)S(1)}, bf16[1024,384]{1,0:T(8,128)(2,1)}, bf16[1024,384]{1,0:T(8,128)(2,1)}, ...), branch_computations={%region_15.18_spmd, %region_18.21_spmd, %region_21.24_spmd} | conditional | flops 824182272 | bytes 40945688
  96.2 53.3 %all-reduce.14.cloned.1.call-done = (f32[1024,768]{1,0:T(8,128)}, f32[1024,768]{1,0:T(8,128)}) async-done(((f32[1024,768]{1,0:T(8,128)}, f32[1024,768]{1,0:T(8,128)}), (f32[1024,768]{1,0:T(8,128)}, f32[1024,768]{1,0:T(8,128)})) %all-reduce.14.cloned.1.call-update) | async-done | bytes 6291472 | tf_op jit(solution)/shard_map/psum | solution.py:426
  157.4 5.1 multiply_convert_fusion.10
  162.6 4.3 fusion.184
  166.9 10.3 %fusion.149 = f32[1024,768]{1,0:T(8,128)} fusion(bf16[1536,768]{1,0:T(8,128)(2,1)} %param.59, bf16[768,1536]{1,0:T(8,128)(2,1)} %param.57, f32[1536]{0:T(1024)S(1)} %copy-done.52, f32[768]{0:T(1024)S(1)} %copy-done.39, f32[768]{0:T(1024)S(1)} %copy-done.40, f32[1024]{0:T(1024)S(1)} %get-tuple-element.328, f32[1024]{0:T(1024)S(1)} %broadcast_multiply_fusion.5, ...), kind=kOutput, calls=%fused_computation.238 | convolution fusion | flops 4847566848 | bytes 12606464 | tf_op jit(solution)/shard_map/dot_general | solution.py:485
  177.5 33.2 %all-reduce.12.cloned.1.call-done = (f32[1024,768]{1,0:T(8,128)}, f32[1024,768]{1,0:T(8,128)}) async-done(((f32[1024,768]{1,0:T(8,128)}, f32[1024,768]{1,0:T(8,128)}), (f32[1024,768]{1,0:T(8,128)}, f32[1024,768]{1,0:T(8,128)})) %all-reduce.12.cloned.1.call-update) | async-done | bytes 6291472 | tf_op jit(solution)/shard_map/psum | solution.py:426
  210.7 4.2 fusion.167
  223.9 5.4 %convert_reduce_fusion.6 = (f32[1536]{0:T(1024)S(1)}, bf16[1024,1536]{1,0:T(8,128)(2,1)S(1)}) fusion(bf16[1536,768]{1,0:T(8,128)(2,1)S(1)} %copy-done.48, f32[1024,768]{1,0:T(8,128)S(1)} %get-tuple-element.263, f32[1024,1536]{1,0:T(8,128)S(1)} %bitcast.400, f32[1536]{0:T(1024)S(1)} %copy-done.53), kind=kOutput, calls=%fused_computation.186 | convolution fusion | flops 2441869824 | bytes 14954496 | tf_op jit(solution)/shard_map/dot_general | solution.py:331
  231.1 4.3 fusion.185
  235.7 8.2 %convolution_dynamic-update-slice_fusion.1 = f32[768,4608]{1,0:T(8,128)} fusion(bf16[1024,1536]{1,0:T(8,128)(2,1)} %copy-done.23, f32[1024,768]{1,0:T(8,128)} %copy-done.12), kind=kOutput, calls=%fused_computation.192 | convolution fusion | flops 2416705536 | bytes 11010048 | tf_op jit(solution)/shard_map/dot_general | solution.py:337
  244.0 4.6 convolution_dynamic-update-slice_fusion
  248.6 11.4 %all-reduce.8.cloned.1.call-done = f32[1024,768]{1,0:T(8,128)} async-done(((f32[1024,768]{1,0:T(8,128)}), f32[1024,768]{1,0:T(8,128)}) %all-reduce.8.cloned.1.call-update) | async-done | bytes 3145744 | tf_op jit(solution)/shard_map/psum | solution.py:612
  260.0 4.8 multiply_reduce_fusion.4
  268.7 58.0 %conditional.13 = (f32[384]{0:T(512)S(1)}, f32[384]{0:T(512)S(1)}, bf16[1024,384]{0,1:T(8,128)(2,1)}, bf16[1024,384]{0,1:T(8,128)(2,1)S(1)}, bf16[1024,384]{0,1:T(8,128)(2,1)}) conditional(s32[]{:T(128)} %bitcast.33, (s32[1,8]{1,0:T(1,128)S(1)}, bf16[1024,384]{1,0:T(8,128)(2,1)S(1)}, bf16[1024,384]{1,0:T(8,128)(2,1)S(1)}, ...), branch_computations={%region_38.0_spmd, %region_42.0_spmd, %region_46.50_spmd} | conditional | flops 2063984896 | bytes 152704096
  270.2 10.2 %reshape.470 = bf16[4,256,6,64]{1,0,3,2:T(4,128)(2,1)} reshape(bf16[1024,384]{0,1:T(8,128)(2,1)} %copy.205) | data formatting | bytes 1572864 | tf_op jit(solution)/shard_map/cond/branch_1_fun/reshape | solution.py:346
  283.5 4.8 fusion.113
  290.1 4.3 multiply_reduce_fusion.1
  305.4 4.5 convert_reduce_fusion.2
  344.4 16.5 %reshape.483 = f32[4,2,2,48,18,256]{5,4,3,2,1,0:T(8,128)} reshape(f32[768,4608]{1,0:T(8,128)} %fusion.145) | data formatting | bytes 28311552 | tf_op jit(solution)/shard_map/reshape | solution.py:304
  360.9 17.2 %copy.407 = f32[4,2,2,48,18,256]{5,3,2,1,0,4:T(8,128)} copy(f32[4,2,2,48,18,256]{5,4,3,2,1,0:T(8,128)} %reshape.483) | data formatting | bytes 28311552 | tf_op jit(solution)/shard_map/reshape | solution.py:304
  378.1 140.3 %shard_map.443 = (f32[48,4608]{1,0:T(8,128)}, f32[8,896]{1,0:T(8,128)}) custom-call(f32[18,4,2,2,48,256]{5,4,3,2,1,0:T(8,128)} %bitcast.311, f32[8,896]{1,0:T(8,128)} %reshape.484.small), custom_call_target="tpu_custom_call" | custom-call | tf_op jit(solution)/shard_map/pallas_call | solution.py:285
  524.7 4.9 add.260
  (223 shorter events, 133.3 us)
Async XLA Ops:
  7.2 150.0 %copy-start = (bf16[768,1536]{1,0:T(8,128)(2,1)S(1)}, bf16[768,1536]{1,0:T(8,128)(2,1)}, u32[]{:S(2)}) copy-start(bf16[768,1536]{1,0:T(8,128)(2,1)} %param.72) | copy-start | bytes 7077892
  7.2 142.2 %all-reduce.14.cloned.1.call-start = ((), (), s32[]{:S(2)}) async-start(), calls=%async_computation.3 | async-start | bytes 12582912 | tf_op jit(solution)/shard_map/psum | solution.py:426
  96.1 53.4 %copy-start.34 = (f32[768]{0:T(1024)S(1)}, f32[768]{0:T(1024)}, u32[]{:S(2)}) copy-start(f32[768]{0:T(1024)} %param.54) | copy-start | bytes 9220
  96.1 56.3 %copy-start.38 = (f32[768]{0:T(1024)S(1)}, f32[768]{0:T(1024)}, u32[]{:S(2)}) copy-start(f32[768]{0:T(1024)} %param.69) | copy-start | bytes 9220
  96.1 114.6 %all-reduce.12.cloned.1.call-start = ((), (), s32[]{:S(2)}) async-start(), calls=%async_computation.2 | async-start | bytes 12582912 | tf_op jit(solution)/shard_map/psum | solution.py:426
  156.6 6.0 %copy-start.2 = (f32[1024,768]{1,0:T(8,128)}, f32[1024,768]{1,0:T(8,128)S(1)}, u32[]{:S(2)}) copy-start(f32[1024,768]{1,0:T(8,128)S(1)} %get-tuple-element.274) | copy-start | bytes 9437188
  157.4 5.1 copy-start.47
  162.6 4.3 copy-start.23
  162.6 4.3 copy-start.39
  162.6 4.3 copy-start.40
  162.6 4.3 copy-start.52
  177.2 33.5 %copy-start.41 = (f32[768]{0:T(1024)S(1)}, f32[768]{0:T(1024)}, u32[]{:S(2)}) copy-start(f32[768]{0:T(1024)} %param.60) | copy-start | bytes 9220
  177.2 82.8 %all-reduce.8.cloned.1.call-start = ((), (), s32[]{:S(2)}) async-start(), calls=%async_computation | async-start | bytes 6291456 | tf_op jit(solution)/shard_map/psum | solution.py:612
  210.7 4.8 copy-start.24
  217.9 5.5 %slice-start = ((s8[6291456]{0:T(1024)(128)(4,1)}), s8[4194304]{0:T(1024)(128)(4,1)S(1)}, s32[]{:S(2)}) async-start(s8[6291456]{0:T(1024)(128)(4,1)} %bitcast.399), calls=%async_computation.4 | async-start | bytes 8388608
  218.6 4.9 slice-start.1
  223.4 6.0 %copy-start.12 = (f32[1024,768]{1,0:T(8,128)}, f32[1024,768]{1,0:T(8,128)S(1)}, u32[]{:S(2)}) copy-start(f32[1024,768]{1,0:T(8,128)S(1)} %get-tuple-element.263) | copy-start | bytes 9437188
  235.4 289.3 %all-reduce.10.cloned.1.call-start = ((), (), s32[]{:S(2)}) async-start(), calls=%async_computation.1 | async-start | bytes 6291456 | tf_op jit(solution)/shard_map/psum | solution.py:639
  235.7 8.3 %copy-start.4 = (f32[1024,768]{1,0:T(8,128)S(1)}, f32[1024,768]{1,0:T(8,128)}, u32[]{:S(2)}) copy-start(f32[1024,768]{1,0:T(8,128)} %copy-done.2) | copy-start | bytes 9437188
  235.7 8.3 %copy-start.59 = (bf16[1024,1536]{1,0:T(8,128)(2,1)S(1)}, bf16[1024,1536]{1,0:T(8,128)(2,1)}, u32[]{:S(2)}) copy-start(bf16[1024,1536]{1,0:T(8,128)(2,1)} %copy-done.58) | copy-start | bytes 9437188
  260.0 4.9 copy-start.5
  333.1 4.9 copy-start.18
  333.1 4.9 copy-start.25
  522.7 7.0 %copy-start.1 = (bf16[768,1536]{1,0:T(8,128)(2,1)S(1)}, bf16[768,1536]{1,0:T(8,128)(2,1)}, u32[]{:S(2)}) copy-start(bf16[768,1536]{1,0:T(8,128)(2,1)} %param.72) | copy-start | bytes 7077892
  (35 other events, 71.8 us)
Sparse Core Ops, SparseCore 0:
  96.2 53.1 all-reduce.13
  177.3 33.3 all-reduce.11
  235.6 24.3 all-reduce.7
  333.2 32.8 all-reduce.9
